TPU v7x, 128 devices: a whole 4x4x4 slice. The times are simulated.
128 devices in a mesh: section: 2 (over y_hi), fsdp: 64 (over x, y_lo, z, core).
Axes of the slice: x: 4, y: 4 (y_hi: 2, y_lo: 2; y = y_hi * 2 + y_lo), z: 4, core: 2. Of those that a mesh axis runs over, the one named last changes fastest.
Arguments:
- tokens_in: bfloat16 [2, 64, 128, 896], P(None, 'fsdp'), may hold values from -6 to 6
- out_grad: bfloat16 [2, 64, 128, 896], P(None, 'fsdp'), may hold values from -6 to 6
- segments: int32 [2, 64, 128], P(None, 'fsdp'), may hold values from 0 to 3, never falling along the last dimension, each value on 1 to 64 neighbouring positions
- norm1_gain: bfloat16 [2, 896], P('section', 'fsdp'), may hold values from 0.099609375 to 1.8984375
- qkv_weight: bfloat16 [2, 896, 1152], P('section', 'fsdp'), may hold values from -0.1875 to 0.1875
- qkv_bias: bfloat16 [2, 1152], P('section', 'fsdp'), may hold values from -3 to 3
- out_weight: bfloat16 [2, 896, 896], P('section', 'fsdp'), may hold values from -0.75 to 0.75
- norm2_gain: bfloat16 [2, 896], P('section', 'fsdp'), may hold values from 0.099609375 to 1.8984375
- gate_weight: bfloat16 [2, 896, 4864], P('section', 'fsdp'), may hold values from -0.1875 to 0.1875
- up_weight: bfloat16 [2, 896, 4864], P('section', 'fsdp'), may hold values from -0.1875 to 0.1875
- down_weight: bfloat16 [2, 4864, 896], P('section', 'fsdp'), may hold values from -0.078125 to 0.078125
Outputs:
- section_out: bfloat16 [2, 2, 64, 128, 896], P('section', None, 'fsdp')
- section_in_grad: bfloat16 [2, 2, 64, 128, 896], P('section', None, 'fsdp')
- norm1_gain_grad: float32 [2, 896], P('section', 'fsdp')
- qkv_weight_grad: float32 [2, 896, 1152], P('section', 'fsdp')
- qkv_bias_grad: float32 [2, 1152], P('section', 'fsdp')
- out_weight_grad: float32 [2, 896, 896], P('section', 'fsdp')
- norm2_gain_grad: float32 [2, 896], P('section', 'fsdp')
- gate_weight_grad: float32 [2, 896, 4864], P('section', 'fsdp')
- up_weight_grad: float32 [2, 896, 4864], P('section', 'fsdp')
- down_weight_grad: float32 [2, 4864, 896], P('section', 'fsdp')
Inputs may be any that keep to these rules, and one draw needn't show every extreme that they name: `segments`: along each sequence the segment numbers never fall; a document covers at most 64 tokens of its sequence, and some document covers exactly that many.
All inputs are finite; a program needn't handle non-finite values.
Results may differ from a plain program's by a relative error of at most 0.023.
Values may be sent and summed in bfloat16 or wider, within the bound.
A program may use at most 192 MiB of HBM per device.

v0:
```python
import math
from types import SimpleNamespace

import jax
import jax.numpy as jnp
from jax import lax
from jax.experimental import pallas as pl
from jax.experimental.pallas import tpu as pltpu
from jax.sharding import PartitionSpec as P
import numpy as np

HEADS = 14
KV_HEADS = 2
HEAD_DIM = 64
MICRO = 2
SEQ = 128
D = 896
DP = 1024
QKV = 1152
norm_epsilon = 1e-06
rope_base = 1000000.0

MESH = pl.DeviceIdType.MESH
BF = jnp.bfloat16
F32 = jnp.float32


class Peer:
    def __init__(self, id, link):
        self.id, self.link = id, link


class Place:
    def __init__(self):
        f = lax.axis_index("fsdp")
        self.s = lax.axis_index("section")
        self.c = lax.rem(f, 2)
        self.z = lax.rem(f // 2, 4)
        self.y = lax.rem(f // 8, 2)
        self.x = f // 16

    def at(self, s=None, x=None, y=None, z=None, c=None):
        s = self.s if s is None else s
        x = self.x if x is None else x
        y = self.y if y is None else y
        z = self.z if z is None else z
        c = self.c if c is None else c
        return (s, ((x * 2 + y) * 4 + z) * 2 + c)

    def step(self, axis, k):
        here = self.x if axis == "x" else self.z
        return lax.rem(here + (k + 4), 4)

    def to(self, axis, k):
        return Peer(self.at(**{axis: self.step(axis, k)}), (axis, k))

    def across(self):
        return Peer(self.at(y=1 - self.y), "y")

    def mate(self):
        return Peer(self.at(c=1 - self.c), "mate")

    def beyond(self):
        return Peer(self.at(s=1 - self.s, y=1 - self.y), "section")


def greet(place):
    barrier = pltpu.get_barrier_semaphore()
    near = (
        place.to("x", 1), place.to("x", -1), place.to("z", 1), place.to("z", -1),
        place.across(), place.mate(), place.beyond(),
    )
    for peer in near:
        pl.semaphore_signal(barrier, inc=1, device_id=peer.id, device_id_type=MESH)
    pl.semaphore_wait(barrier, len(near))


RATE = {"mate": 150e3}
LINK_RATE = 48e3
LATENCY = 1.5


class Wire:
    def __init__(self, send_sems, recv_sems):
        self.send_sems, self.recv_sems = send_sems, recv_sems
        self.count, self.started, self.flows = 0, [], []
        self.now, self.free = 0.0, {}

    def send(self, src, dst, peer):
        k = self.count
        self.count += 1
        assert k < self.send_sems.shape[0]
        copy = pltpu.make_async_remote_copy(
            src_ref=src, dst_ref=dst, send_sem=self.send_sems.at[k],
            recv_sem=self.recv_sems.at[k], device_id=peer.id, device_id_type=MESH,
        )
        copy.start()
        self.started.append(copy)
        size = 2 * math.prod(dst.shape)
        begin = max(self.now, self.free.get(peer.link, 0.0))
        self.free[peer.link] = begin + size / RATE.get(peer.link, LINK_RATE)
        copy.there = self.free[peer.link] + LATENCY
        return copy

    def drain(self):
        for copy in self.started:
            copy.wait_send()
        self.started = []

    def add(self, flow):
        self.flows.append([None, flow])
        self.go_on(self.flows[-1])

    def go_on(self, entry):
        try:
            entry[0] = next(entry[1])
        except StopIteration:
            self.flows.remove(entry)

    def run(self):
        while self.flows:
            times = [(entry[0](), k) for k, entry in enumerate(self.flows)]
            when, k = min((t, k) for t, k in times if t is not None)
            self.now = max(self.now, when)
            self.go_on(self.flows[k])

    def busy(self, us):
        self.now += us


def got(*copies):
    yield lambda: max(copy.there for copy in copies)
    for copy in copies:
        copy.wait_recv()


def until(condition):
    yield lambda: 0.0 if condition() else None


def ring(wire, place, axis, piece, spawn):
    me = place.x if axis == "x" else place.z
    before, after, far = place.step(axis, -1), place.step(axis, 1), place.step(axis, 2)
    r = wire.send(piece(me), piece(me), place.to(axis, 1))
    l = wire.send(piece(me), piece(me), place.to(axis, -1))
    last = []

    def right():
        yield from got(r)
        last.append(wire.send(piece(before, 0), piece(before, 0), place.to(axis, 1)))
        spawn(before)

    def left():
        yield from got(l)
        last.append(wire.send(piece(after, 1), piece(after, 1), place.to(axis, -1)))
        spawn(after)

    def rest():
        yield from until(lambda: len(last) == 2)
        yield from got(*last)
        spawn(far)

    for flow in (right(), left(), rest()):
        wire.add(flow)


def gather_yab(wire, place, slot, first, last, finished):
    x, y, z = place.x, place.y, place.z
    cross = wire.send(slot(x, y, z), slot(x, y, z), place.across())
    yield from got(cross)
    mine = {"x": x, "z": z}
    count = []

    def piece(a, b, half=None):
        return slot(b, half, a) if first == "z" else slot(a, half, b)

    def arrived(b):
        count.append(b)
        if len(count) == 16:
            finished()

    def along_last(a):
        arrived(a)
        ring(wire, place, last, lambda b, half=None: piece(a, b, half), arrived)

    ring(wire, place, first, lambda a, half=None: piece(a, mine[last], half), along_last)
    along_last(mine[first])


def gather_down(wire, place, D, finished):
    x, y, z = place.x, place.y, place.z
    count = []

    def by_x(a, half=None):
        if half is None:
            return D.at[a, y, z]
        return D.at[a, y, z, pl.ds(0, 48) if half == 0 else pl.ds(48, 32)]

    def by_z(b, half=None):
        if half is None:
            return D.at[:, y, b]
        return D.at[pl.ds(2 * half, 2), y, b]

    def along_y(b):
        cross = wire.send(by_z(b), by_z(b), place.across())

        def arrival():
            yield from got(cross)
            count.append(b)
            if len(count) == 4:
                finished()

        wire.add(arrival())

    def x_done(a):
        seen.append(a)
        if len(seen) == 3:
            ring(wire, place, "z", by_z, along_y)
            along_y(z)

    seen = []
    ring(wire, place, "x", by_x, x_done)


BLOCK = dict(G=(32, 2560), U=(32, 2560), D=(80, 896), Q=(32, 1152), O=(32, 896))


def start_gather(wire, place, ins, bufs, local_sems, done):
    x, y, z, c = place.x, place.y, place.z, place.c
    rows = pl.ds(pl.multiple_of(c * 16, 16), 16)
    G, U, D, Q, O = bufs
    g_in, u_in, d_in, q_in, o_in = ins
    own = {}
    for k, (name, src, dst) in enumerate((
        ("Q", q_in, Q.at[x, y, z, rows]), ("O", o_in, O.at[x, y, z, rows]), ("D", d_in, D.at[x, y, z]),
        ("G", g_in.at[c], G.at[x, y, z, rows]), ("U", u_in.at[c], U.at[x, y, z, rows]),
    )):
        own[name] = pltpu.make_async_copy(src, dst, local_sems.at[k])
        own[name].start()
    swap_g = wire.send(g_in.at[1 - c], G.at[x, y, z, rows], place.mate())
    swap_u = wire.send(u_in.at[1 - c], U.at[x, y, z, rows], place.mate())

    def whole(buf):
        def slot(px, half, pz):
            if half is None:
                return buf.at[px, :, pz]
            return buf.at[px, half, pz]
        return slot

    def part(buf):
        def slot(px, half, pz):
            if half is None:
                return buf.at[px, :, pz, rows]
            return buf.at[px, half, pz, rows]
        return slot

    def attention(name, buf):
        own[name].wait()
        filled = []
        yield from gather_yab(wire, place, part(buf), "z", "x", lambda: filled.append(1))
        yield from until(lambda: filled)
        mine = buf.at[:, :, :, rows]
        swap = wire.send(mine, mine, place.mate())
        yield from got(swap)
        done.add(name)

    def hidden(name, buf, swap, first, last):
        yield from got(swap)
        own[name].wait()
        yield from gather_yab(wire, place, whole(buf), first, last, lambda: done.add(name))

    wire.add(attention("Q", Q))
    wire.add(attention("O", O))
    own["D"].wait()
    gather_down(wire, place, D, lambda: done.add("D"))
    wire.add(hidden("G", G, swap_g, "z", "x"))
    wire.add(hidden("U", U, swap_u, "x", "z"))


def bufs_shapes():
    return [(4, 2, 4) + BLOCK[k] for k in "GUDQO"]


def add(dst, *srcs):
    total = dst[...]
    for src in srcs:
        total = total + src[...]
    dst[...] = total


def add_each(count, dst, *srcs):
    def body(i, carry):
        add(dst(i), *[src(i) for src in srcs])
        return carry
    lax.fori_loop(0, count, body, 0)


def scatter_ring(wire, place, axis, piece, land, halves, finished):
    me = place.x if axis == "x" else place.z
    before, after, far = place.step(axis, -1), place.step(axis, 1), place.step(axis, 2)
    l1a, l1b, l2a, l2b = land
    r = wire.send(piece(far, 0), l1a, place.to(axis, 1))
    l = wire.send(piece(far, 1), l1b, place.to(axis, -1))
    last = []

    def right():
        yield from got(r)
        add(piece(after, 0), l1a)
        last.append(wire.send(piece(after), l2a, place.to(axis, 1)))

    def left():
        yield from got(l)
        add(piece(before, 1), l1b)
        last.append(wire.send(piece(before), l2b, place.to(axis, -1)))

    def rest():
        yield from until(lambda: len(last) == 2)
        yield from got(*last)
        halves(lambda i: piece(me, i), l2a, l2b)
        finished()

    for flow in (right(), left(), rest()):
        wire.add(flow)


def two_halves(dst, a, b):
    for i in range(2):
        add(dst(i), a.at[i], b.at[i])


def scatter_aby(wire, place, slot, R, first, last):
    r1a, r1b, r2a, r2b, s1a, s1b, s2a, s2b, t_buf = R
    mine = {"x": place.x, "z": place.z}

    def piece(a, b, half=None):
        return slot(b, half, a) if first == "z" else slot(a, half, b)

    order = [place.step(last, k) for k in (2, 1, -1)] + [mine[last]]
    filled = []
    for k, b in enumerate(order):
        scatter_ring(
            wire, place, first, lambda a, half=None, b=b: piece(a, b, half),
            (r1a.at[k], r1b.at[k], r2a.at[k], r2b.at[k]), two_halves, lambda k=k: filled.append(k),
        )
    a0 = mine[first]
    bq, bp, bm, b0 = order
    sent = []

    def outer():
        yield from until(lambda: 0 in filled)
        d_r = wire.send(piece(a0, bq, 0), s1a, place.to(last, 1))
        d_l = wire.send(piece(a0, bq, 1), s1b, place.to(last, -1))

        def right():
            yield from until(lambda: 1 in filled)
            yield from got(d_r)
            add(piece(a0, bp, 0), s1a)
            sent.append(wire.send(piece(a0, bp), s2a, place.to(last, 1)))

        def left():
            yield from until(lambda: 2 in filled)
            yield from got(d_l)
            add(piece(a0, bm, 1), s1b)
            sent.append(wire.send(piece(a0, bm), s2b, place.to(last, -1)))

        wire.add(right())
        wire.add(left())

    wire.add(outer())
    yield from until(lambda: len(sent) == 2 and 3 in filled)
    yield from got(*sent)
    two_halves(lambda i: piece(a0, b0, i), s2a, s2b)
    cross = wire.send(slot(place.x, 1 - place.y, place.z), t_buf, place.across())
    yield from got(cross)
    add(slot(place.x, place.y, place.z), t_buf)


def scatter_down(wire, place, D, R):
    yb, z1a, z1b, z2a, z2b, xa, xb, x2a, x2b = R
    x, y, z = place.x, place.y, place.z
    zp, zm, zq = place.step("z", 1), place.step("z", -1), place.step("z", 2)
    order = (zq, zp, zm, z)
    crossing = [wire.send(D.at[:, 1 - y, b], yb.at[k], place.across()) for k, b in enumerate(order)]
    sent = []

    def settle(k):
        yield from got(crossing[k])
        add_each(4, lambda i: D.at[i, y, order[k]], lambda i: yb.at[k, i])

    yield from settle(0)
    d_r = wire.send(D.at[pl.ds(0, 2), y, zq], z1a, place.to("z", 1))
    d_l = wire.send(D.at[pl.ds(2, 2), y, zq], z1b, place.to("z", -1))

    def right():
        yield from settle(1)
        yield from got(d_r)
        add_each(2, lambda i: D.at[i, y, zp], lambda i: z1a.at[i])
        sent.append(wire.send(D.at[:, y, zp], z2a, place.to("z", 1)))

    def left():
        yield from settle(2)
        yield from got(d_l)
        add_each(2, lambda i: D.at[i + 2, y, zm], lambda i: z1b.at[i])
        sent.append(wire.send(D.at[:, y, zm], z2b, place.to("z", -1)))

    wire.add(right())
    wire.add(left())
    yield from settle(3)
    yield from until(lambda: len(sent) == 2)
    yield from got(*sent)
    add_each(4, lambda i: D.at[i, y, z], lambda i: z2a.at[i], lambda i: z2b.at[i])

    def by_x(a, half=None):
        if half is None:
            return D.at[a, y, z]
        return D.at[a, y, z, pl.ds(0, 48) if half == 0 else pl.ds(48, 32)]

    ended = []
    scatter_ring(
        wire, place, "x", by_x, (xa, xb, x2a, x2b),
        lambda dst, a, b: add(D.at[x, y, z], a, b), lambda: ended.append(1),
    )
    yield from until(lambda: ended)


def rs_scratch():
    def aby(rows, cols):
        shapes = [(4, rows, cols)] * 2 + [(4, 2, rows, cols)] * 2 + [(rows, cols)] * 2 + [(2, rows, cols)] * 2 + [(rows, cols)]
        return [pltpu.VMEM(s, BF) for s in shapes]
    out = []
    out += aby(32, 2560) + [pltpu.VMEM((16, 2560), BF)]
    out += aby(32, 2560) + [pltpu.VMEM((16, 2560), BF)]
    b = (80, 896)
    out += [pltpu.VMEM(s, BF) for s in (
        (4, 4) + b, (2,) + b, (2,) + b, (4,) + b, (4,) + b, (48, 896), (32, 896), b, b)]
    out += aby(16, 1152) + [pltpu.VMEM((4, 2, 4, 16, 1152), BF)]
    out += aby(16, 896) + [pltpu.VMEM((4, 2, 4, 16, 896), BF)]
    return out


N_RS_SCRATCH = 10 + 10 + 9 + 10 + 10


def start_scatter(wire, place, bufs, R, made, end):
    x, y, z, c = place.x, place.y, place.z, place.c
    G, U, D, Q, O = bufs
    rg, ru, rd, rq, ro = R[:10], R[10:20], R[20:29], R[29:39], R[39:49]
    rows = pl.ds(pl.multiple_of(c * 16, 16), 16)
    others = pl.ds(pl.multiple_of(16 - c * 16, 16), 16)

    def whole(buf):
        def slot(px, half, pz):
            return buf.at[px, :, pz] if half is None else buf.at[px, half, pz]
        return slot

    def part(buf):
        def slot(px, half, pz):
            return buf.at[px, :, pz, rows] if half is None else buf.at[px, half, pz, rows]
        return slot

    def hidden(name, buf, r, first, last):
        yield from until(lambda: name in made)
        yield from scatter_aby(wire, place, whole(buf), r[:9], first, last)
        swap = wire.send(buf.at[x, y, z, others], r[9], place.mate())
        yield from got(swap)
        end(name, c, buf[x, y, z, rows], r[9][...])

    def attention(name, buf, r):
        yield from until(lambda: name in made)
        swap = wire.send(buf.at[:, :, :, others], r[9], place.mate())
        yield from got(swap)
        add_each(32, lambda i: buf.at[i // 8, lax.rem(i // 4, 2), lax.rem(i, 4), rows],
                 lambda i: r[9].at[i // 8, lax.rem(i // 4, 2), lax.rem(i, 4)])
        yield from scatter_aby(wire, place, part(buf), r[:9], "x", "z")
        end(name, c, buf[x, y, z, rows])

    def down():
        yield from until(lambda: "D" in made)
        yield from scatter_down(wire, place, D, rd)
        end("D", c, D[x, y, z])

    wire.add(down())
    wire.add(hidden("G", G, rg, "x", "z"))
    wire.add(hidden("U", U, ru, "z", "x"))
    wire.add(attention("O", O, ro))
    wire.add(attention("Q", Q, rq))


TOK = 256
FF = 2560


def mm(a, b):
    return jnp.dot(a, b, preferred_element_type=F32)


def mm_t(a, b):
    return lax.dot_general(a, b, (((1,), (1,)), ((), ())), preferred_element_type=F32)


def t_mm(a, b):
    return lax.dot_general(a, b, (((0,), (0,)), ((), ())), preferred_element_type=F32)


def constants():
    d = np.arange(D)
    spread = np.zeros((D, DP), np.float32)
    spread[d, 16 * (d // 14) + d % 14] = 1
    pick = np.zeros((64, DP), np.float32)
    pick[np.arange(64), 16 * np.arange(64) + 14] = 1
    own14 = (np.arange(64)[:, None] == d[None] // 14).astype(np.float32)
    j = np.arange(QKV)
    own18 = (np.arange(64)[:, None] == j[None] // 18).astype(np.float32)
    lane = np.arange(128)[:, None]
    e1 = (lane == d[None] % 14).astype(np.float32)
    eb = (lane == 64 + j[None] % 18).astype(np.float32)
    return [jnp.asarray(a, BF) for a in (spread, pick, own14, own18, e1, eb)]


CONST = ("spread", "pick", "own14", "own18", "e1", "eb")


def cols(buf, start, size):
    value = buf[:, :, :, :, pl.ds(start, size)]
    return value.reshape(-1, size)


def put(ref, value):
    ref[...] = value.reshape(ref.shape)


def rotate(x, lo32):
    return jnp.where(lo32, pltpu.roll(x, 96, 1), pltpu.roll(x, 32, 1))


def lane_is(shape, width, below):
    lane = lax.broadcasted_iota(jnp.int32, shape, 1)
    return lax.rem(lane, width) < below


def gains(R):
    q = cols(R.Q, 0, 128)
    s = mm(R.pick[...], q)
    s2 = pltpu.roll(s, 96, 1).astype(BF)
    s = s.astype(BF)
    R.g1[...] = jnp.sum(mm(s, R.e1[...]) * R.own14[...].astype(F32), axis=0, keepdims=True)
    R.g2[...] = jnp.sum(mm(s2, R.e1[...]) * R.own14[...].astype(F32), axis=0, keepdims=True)
    R.bias[...] = jnp.sum(mm(s, R.eb[...]) * R.own18[...].astype(F32), axis=0, keepdims=True)


def inverse_rms(h):
    return lax.rsqrt(jnp.sum(h * h, axis=-1, keepdims=True) * (1.0 / D) + norm_epsilon)


def project_qkv(R, source, tables, rows, size):
    h = source[rows].astype(F32)
    n1 = (h * inverse_rms(h) * R.g1[...]).astype(BF)
    R.N1[rows] = mm(n1, R.spread[...]).astype(BF)
    lo32 = lane_is((size, 128), 64, 32)
    lo = lane_is((size, 128), 128, 64)
    cos, sin = tables[0][rows], tables[1][rows]
    for start, width in ((0, 256), (256, 256), (512, 256), (768, 256), (1024, 128)):
        out = mm(R.N1[rows], cols(R.Q, start, width)) + R.bias[:, start:start + width]
        for k in range(width // 128):
            x = out[:, 128 * k:128 * k + 128]
            tile = (start + 128 * k) // 128
            if tile < 8:
                x = x * cos + rotate(x, lo32) * sin
            if tile < 7:
                R.QR[rows, 128 * tile:128 * tile + 128] = x.astype(BF)
            else:
                x = x.astype(BF).astype(F32)
                swapped = pltpu.roll(x, 64, 1)
                R.KV[tile - 7, 0, rows] = jnp.where(lo, x, swapped).astype(BF)
                R.KV[tile - 7, 1, rows] = x.astype(BF)
                R.KV[tile - 7, 2, rows] = jnp.where(lo, swapped, x).astype(BF)


def two_heads(R, tile):
    return jnp.concatenate([tile * R.lanes[0], tile * R.lanes[1]], axis=0)


def beside(x):
    return jnp.concatenate([x[:SEQ], x[SEQ:]], axis=1)


def variant_of(t):
    return 0 if t < 3 else (2 if t > 3 else 1)


def probs_of(R, mask, t, rows):
    q2 = two_heads(R, R.QR[rows, 128 * t:128 * t + 128])
    kk = R.KV[0, variant_of(t), rows]
    s = mm_t(q2, kk) * 0.125 + jnp.concatenate([mask, mask], axis=0)
    e = jnp.exp(s - jnp.max(s, axis=-1, keepdims=True))
    p = e * (1.0 / jnp.sum(e, axis=-1, keepdims=True))
    return q2, kk, p


def attend(R, tables, m):
    rows = own_rows(m)
    mask = tables[2][m]
    for t in range(7):
        _, _, p = probs_of(R, mask, t, rows)
        vv = two_heads(R, R.KV[1, variant_of(t), rows])
        R.DQKV[rows, 128 * t:128 * t + 128] = mm(beside(p.astype(BF)), vv).astype(BF)


def own_rows(m):
    return pl.ds(SEQ * m, SEQ)


def pair_own(m):
    return pl.ds(2 * SEQ * m, SEQ)


def pair_other(m):
    return pl.ds(2 * SEQ * m + SEQ, SEQ)


def pair(m):
    return pl.ds(2 * SEQ * m, 2 * SEQ)


def after_attention(R, source, m):
    rows = own_rows(m)
    R.CP[rows] = mm(R.DQKV[rows, :D], R.spread[...]).astype(BF)
    mid = source[rows].astype(F32) + mm(R.CP[rows], cols(R.O, 0, D))
    R.MID[rows] = mid
    n2 = (mid * inverse_rms(mid) * R.g2[...]).astype(BF)
    R.N2[pair_own(m)] = mm(n2, R.spread[...]).astype(BF)


def sigmoid(v):
    return 0.5 * jnp.tanh(0.5 * v) + 0.5


def hidden(R, m):
    rows = pair(m)

    def body(j, carry):
        at = pl.ds(pl.multiple_of(j * 256, 256), 256)
        n2 = R.N2[rows]
        gate = mm(n2, R.G[:, :, :, :, at].reshape(DP, 256))
        up = mm(n2, R.U[:, :, :, :, at].reshape(DP, 256))
        R.GA[rows, at] = gate.astype(BF)
        R.UP[rows, at] = up.astype(BF)
        R.ACT[rows, at] = (gate * sigmoid(gate) * up).astype(BF)
        return carry

    lax.fori_loop(0, FF // 256, body, 0)


class Swap:
    def __init__(self, R, place):
        own = own_rows
        mate, across, beyond = place.mate(), place.across(), place.beyond()

        def table(k, refs, device):
            return lambda m: pltpu.make_async_remote_copy(
                src_ref=refs(m)[0], dst_ref=refs(m)[1], send_sem=R.xs.at[2 * k + m],
                recv_sem=R.xr.at[2 * k + m], device_id=device.id, device_id_type=MESH,
            )

        self.n2 = table(0, lambda m: (R.N2.at[pair_own(m)], R.N2.at[pair_other(m)]), mate)
        self.part = table(1, lambda m: (R.DB.at[own(m)], R.DC.at[own(m)]), mate)
        self.dy = table(2, lambda m: (R.DY.at[pair_own(m)], R.DY.at[pair_other(m)]), mate)
        self.dn = table(3, lambda m: (R.dn, R.dn_in.at[own(m)]), mate)
        self.hop_h = table(4, lambda m: (R.ys.at[own(m)], R.h.at[own(m)]), beyond)
        self.hop_dy = table(5, lambda m: (R.dhs.at[own(m)], R.DY.at[pair_own(m)]), beyond)
        self.og = table(6, lambda m: (R.og.at[own(m)], R.DY.at[pair_own(m)]), across)
        self.cos = table(7, lambda m: (R.cos.at[own(m)], R.tcos.at[own(m)]), across)
        self.sin = table(8, lambda m: (R.sin.at[own(m)], R.tsin.at[own(m)]), across)
        self.mask = table(9, lambda m: (R.mask.at[m], R.tmask.at[m]), across)
        self.y = table(10, lambda m: (R.ys.at[own(m)], R.y.at[own(m)]), across)
        self.dh = table(11, lambda m: (R.dhs.at[own(m)], R.dh.at[own(m)]), across)


N_SWAP = 24


def down_sent(R, swap, m):
    R.DB[own_rows(m)] = mm(R.ACT[pair_other(m)], R.D[...].reshape(FF, D)).astype(BF)
    swap.part(m).start()
    R.acc[SEQ:, 0:D] = R.MID[own_rows(m)] + mm(R.ACT[pair_own(m)], R.D[...].reshape(FF, D))


def down_done(R, swap, m):
    swap.part(m).wait_recv()
    R.ys[own_rows(m)] = (R.acc[SEQ:, 0:D] + R.DC[own_rows(m)].astype(F32)).astype(BF)
    swap.part(m).wait_send()


def hidden_back(R, m):
    rows = pair(m)

    def body(j, carry):
        down = R.D[j].reshape(640, D)
        for start, size in ((0, 256), (256, 256), (512, 128)):
            sub = pl.ds(pl.multiple_of(j * 640 + start, 128), size)
            dact = mm_t(R.DY[rows], down[start:start + size])
            gate = R.GA[rows, sub].astype(F32)
            up = R.UP[rows, sub].astype(F32)
            sig = sigmoid(gate)
            R.GA[rows, sub] = (dact * up * sig * (1.0 + gate * (1.0 - sig))).astype(BF)
            R.UP[rows, sub] = (dact * gate * sig).astype(BF)
        return carry

    lax.fori_loop(0, FF // 640, body, 0)


def normed_back(R, swap, m):
    rows = pair(m)
    R.acc[...] = jnp.zeros_like(R.acc)

    def body(j, carry):
        at = pl.ds(pl.multiple_of(j * 512, 512), 512)
        R.acc[...] += mm_t(R.GA[rows, at], R.G[:, :, :, :, at].reshape(DP, 512)) + mm_t(
            R.UP[rows, at], R.U[:, :, :, :, at].reshape(DP, 512)
        )
        return carry

    lax.fori_loop(0, FF // 512, body, 0)
    R.dn[...] = R.acc[SEQ:].astype(BF)
    swap.dn(m).start()


def middle_back(R, swap, m):
    rows = own_rows(m)
    swap.dn(m).wait_recv()
    dn2p = (R.acc[:SEQ] + R.dn_in[rows].astype(F32)).astype(BF)
    dn2 = mm_t(dn2p, R.spread[...])
    mid = R.MID[rows]
    inv2 = inverse_rms(mid)
    R.dg2[m] = jnp.sum(dn2 * mid * inv2, axis=0, keepdims=True)
    scaled = dn2 * R.g2[...]
    mean = jnp.sum(scaled * mid, axis=-1, keepdims=True) * (1.0 / D)
    dmid = R.DY[pair_own(m)].astype(F32) + inv2 * scaled - mid * (inv2 * inv2 * inv2 * mean)
    R.MID[rows] = dmid
    R.DB[rows] = dmid.astype(BF)
    dctx = mm_t(R.DB[rows], cols(R.O, 0, D)).astype(BF)
    R.DC[rows] = mm_t(dctx, R.spread[...]).astype(BF)
    swap.dn(m).wait_send()


def attend_back(R, tables, m):
    rows = own_rows(m)
    cos, sin, mask = tables[0][rows], tables[1][rows], tables[2][m]
    lo32 = lane_is((SEQ, 128), 64, 32)
    lo = lane_is((SEQ, 128), 128, 64)

    def spin_back(g):
        return g * cos + rotate(g * sin, lo32)

    for t in range(7):
        q2, kk, p = probs_of(R, mask, t, rows)
        var = variant_of(t)
        dc2 = two_heads(R, R.DC[rows, 128 * t:128 * t + 128])
        dp = mm_t(dc2, R.KV[1, var, rows])
        ds = (p * (dp - jnp.sum(p * dp, axis=-1, keepdims=True))).astype(BF)
        dk, dv = t_mm(ds, q2), t_mm(p.astype(BF), dc2)
        if t in (0, 3, 4):
            R.dkv[0, var] = dk
            R.dkv[1, var] = dv
        else:
            R.dkv[0, var] += dk
            R.dkv[1, var] += dv
        dq = mm(beside(ds), two_heads(R, kk)) * 0.125
        R.DQKV[rows, 128 * t:128 * t + 128] = spin_back(dq).astype(BF)

    def joined(k):
        first, mixed, last = R.dkv[k, 0], R.dkv[k, 1], R.dkv[k, 2]
        return mixed + jnp.where(
            lo, first + pltpu.roll(first, 64, 1), last + pltpu.roll(last, 64, 1)
        )

    R.DQKV[rows, 896:1024] = spin_back(joined(0) * 0.125).astype(BF)
    R.DQKV[rows, 1024:1152] = joined(1).astype(BF)


def stream_back(R, m):
    rows = own_rows(m)
    dqkv = R.DQKV[rows]
    R.dbias[m] = jnp.sum(dqkv.astype(F32), axis=0, keepdims=True)
    dn1 = mm_t(mm_t(dqkv, cols(R.Q, 0, QKV)).astype(BF), R.spread[...])
    h = R.h[rows].astype(F32)
    inv1 = inverse_rms(h)
    R.dg1[m] = jnp.sum(dn1 * h * inv1, axis=0, keepdims=True)
    scaled = dn1 * R.g1[...]
    mean = jnp.sum(scaled * h, axis=-1, keepdims=True) * (1.0 / D)
    R.dhs[rows] = (R.MID[rows] + inv1 * scaled - h * (inv1 * inv1 * inv1 * mean)).astype(BF)


def pause(wire):
    now = wire.now
    yield lambda: now


def weight_grads(R, wire, done, rest):
    def down(x, carry):
        at = pl.ds(pl.multiple_of(x * 640, 640), 640)
        for start, size in ((0, 512), (512, 384)):
            grad = t_mm(R.ACT[:, at], R.DY[:, start:start + size])
            put(R.D.at[x, :, :, :, pl.ds(start, size)], grad.astype(BF))
        return carry

    lax.fori_loop(0, 4, down, 0)
    done.add("D")
    wire.busy(3.0)
    yield from pause(wire)
    rest[0]()
    wire.busy(4.0)
    for name, buf, grad in (("G", R.G, R.GA), ("U", R.U, R.UP)):
        def tile(x, carry):
            n2 = R.N2[:, pl.ds(pl.multiple_of(x * 256, 256), 256)]
            for start in range(0, FF, 512):
                at = pl.ds(start, 512)
                put(buf.at[x, :, :, :, at], t_mm(n2, grad[:, at]).astype(BF))
            return carry

        yield from pause(wire)
        lax.fori_loop(0, 4, tile, 0)
        done.add(name)
        wire.busy(4.5)
    for piece in rest[1:]:
        yield from pause(wire)
        piece()
        wire.busy(3.0)
    yield from pause(wire)

    def out_rows(x, carry):
        rows = pl.ds(pl.multiple_of(x * 256, 256), 256)
        put(R.O.at[x], t_mm(R.CP[:, rows], R.DB[...]).astype(BF))
        return carry

    lax.fori_loop(0, 4, out_rows, 0)
    done.add("O")
    wire.busy(1.5)
    yield from pause(wire)
    small = (
        mm_t((R.own14[...].astype(F32) * (R.dg1[0] + R.dg1[1])).astype(BF), R.e1[...])
        + pltpu.roll(
            mm_t((R.own14[...].astype(F32) * (R.dg2[0] + R.dg2[1])).astype(BF), R.e1[...]), 32, 1
        )
        + mm_t((R.own18[...].astype(F32) * (R.dbias[0] + R.dbias[1])).astype(BF), R.eb[...])
    )
    R.small[...] = small.astype(BF)

    def qkv_rows(x, carry):
        rows = pl.ds(pl.multiple_of(x * 256, 256), 256)
        n1 = R.N1[:, rows]
        for start in range(0, QKV, 384):
            g = t_mm(n1, R.DQKV[:, start:start + 384])
            if start == 0:
                g = jnp.concatenate([g[:, :128] + t_mm(R.pick[:, rows], R.small[...]), g[:, 128:]], axis=1)
            put(R.Q.at[x, :, :, :, pl.ds(start, 384)], g.astype(BF))
        return carry

    lax.fori_loop(0, 4, qkv_rows, 0)
    done.add("Q")


def pack(R):
    for src, wide, dst in ((R.g_in, R.g_s, R.g_st), (R.u_in, R.g_s, R.u_st)):
        wide[...] = jnp.zeros_like(wide)
        for f in range(64):
            piece = src[:, 76 * f:76 * f + 76].astype(F32)
            wide[f % 2, 0:14, 80 * (f // 2):80 * (f // 2) + 76] = piece
        dst[...] = wide[...].astype(BF)
    R.acc[0:80, 0:D] = jnp.zeros((80, D), F32)
    R.acc[0:76, 0:D] = R.d_in[...].astype(F32)
    R.d_st[...] = R.acc[0:80, 0:D].astype(BF)
    R.o_s[...] = jnp.zeros_like(R.o_s)
    R.o_s[0:14] = R.o_in[...].astype(F32)
    R.o_st[...] = R.o_s[...].astype(BF)
    R.q_s[...] = jnp.zeros_like(R.q_s)
    R.q_s[0:14] = R.q_in[...].astype(F32)
    R.q_s[14:15, 0:14] = R.a_in[...].astype(F32)
    R.q_s[14:15, 32:46] = R.c_in[...].astype(F32)
    R.q_s[14:15, 64:82] = R.b_in[...].astype(F32)
    R.q_st[...] = R.q_s[...].astype(BF)


def unpack(R, name, c, mine, other=None):
    if name in "GU":
        R.g_s[c] = mine.astype(F32)
        R.g_s[1 - c] = other.astype(F32)
        dst = R.g_o if name == "G" else R.u_o
        for f in range(64):
            at = 80 * (f // 2)
            dst[:, 76 * f:76 * f + 76] = R.g_s[f % 2, 0:14, at:at + 76]
    elif name == "D":
        R.acc[0:80, 0:D] = mine.astype(F32)
        R.d_o[...] = R.acc[0:76, 0:D]
    elif name == "O":
        R.o_s[...] = mine.astype(F32)
        R.o_o[...] = R.o_s[0:14]
    else:
        R.q_s[...] = mine.astype(F32)
        R.q_o[...] = R.q_s[0:14]
        R.a_o[...] = R.q_s[14:15, 0:14]
        R.c_o[...] = R.q_s[14:15, 32:46]
        R.b_o[...] = R.q_s[14:15, 64:82]


INS = ("g_in", "u_in", "d_in", "q_in", "o_in", "a_in", "b_in", "c_in", "tokens", "og", "cos", "sin", "mask") + CONST
IN_HBM = ("og", "tokens", "cos", "sin", "mask")
OUTS = ("y", "dh", "g_o", "u_o", "d_o", "q_o", "o_o", "a_o", "b_o", "c_o")
LOCAL = (
    ("h", (TOK, D), BF), ("N1", (TOK, DP), BF), ("QR", (TOK, D), BF),
    ("KV", (2, 3, TOK, 128), BF), ("CP", (TOK, DP), BF),
    ("MID", (TOK, D), F32), ("N2", (2 * TOK, DP), BF), ("GA", (2 * TOK, FF), BF),
    ("UP", (2 * TOK, FF), BF), ("ACT", (2 * TOK, FF), BF), ("DY", (2 * TOK, D), BF), ("acc", (TOK, DP), F32), ("dn", (SEQ, DP), BF), ("dn_in", (TOK, DP), BF),
    ("DB", (TOK, D), BF), ("DC", (TOK, D), BF), ("DQKV", (TOK, QKV), BF),
    ("dkv", (2, 3, SEQ, 128), F32), ("lanes", (2, SEQ, 128), BF),
    ("small", (64, 128), BF),
    ("g1", (1, D), F32), ("g2", (1, D), F32), ("bias", (1, QKV), F32),
    ("dg1", (2, 1, D), F32), ("dg2", (2, 1, D), F32), ("dbias", (2, 1, QKV), F32),
    ("g_st", (2, 16, FF), BF), ("u_st", (2, 16, FF), BF), ("d_st", (80, D), BF),
    ("q_st", (16, QKV), BF), ("o_st", (16, D), BF), ("g_s", (2, 16, FF), F32),
    ("q_s", (16, QKV), F32), ("o_s", (16, D), F32),
    ("ys", (TOK, D), BF), ("dhs", (TOK, D), BF),
    ("tcos", (TOK, 128), F32), ("tsin", (TOK, 128), F32), ("tmask", (2, SEQ, SEQ), F32),
)


def layers_kernel(*refs):
    names = INS + OUTS + tuple("GUDQO") + tuple(name for name, _, _ in LOCAL)
    R = SimpleNamespace(**dict(zip(names, refs)))
    rest = refs[len(names):]
    R.ss, R.rs, R.ls, R.xs, R.xr = rest[N_RS_SCRATCH:]
    place = Place()
    greet(place)
    wire = Wire(R.ss, R.rs)
    swap = Swap(R, place)
    bufs = (R.G, R.U, R.D, R.Q, R.O)
    done = set()
    tables = (R.tcos, R.tsin, R.tmask)

    def only(section):
        return lambda body: pl.when(place.s == section)(body)

    @only(0)
    def _():
        moves = [
            pltpu.make_async_copy(src, dst, R.ls.at[5 + k])
            for k, (src, dst) in enumerate(zip((R.tokens, R.cos, R.sin, R.mask), (R.h,) + tables))
        ]
        for move in moves:
            move.start()
        for move in moves:
            move.wait()

    @only(1)
    def _():
        for m in range(MICRO):
            for move in (swap.og, swap.cos, swap.sin, swap.mask):
                move(m).start()

    def early():
        yield from until(lambda: {"Q", "O"} <= done)
        gains(R)
        only(0)(lambda: project_qkv(R, R.h, tables, pl.ds(0, TOK), TOK))
        wire.busy(2.5)
        for m in range(MICRO):
            yield from pause(wire)
            only(0)(lambda: attend(R, tables, m))
            wire.busy(2.5)
            yield from pause(wire)

            @only(0)
            def _():
                after_attention(R, R.h, m)
                swap.n2(m).start()

            wire.busy(1.5)

    pack(R)
    start_gather(wire, place, (R.g_st, R.u_st, R.d_st, R.q_st, R.o_st), bufs, R.ls, done)
    lo = lane_is((SEQ, 128), 128, 64).astype(F32)
    R.lanes[0] = lo.astype(BF)
    R.lanes[1] = (1.0 - lo).astype(BF)
    wire.add(early())
    wire.run()

    @only(0)
    def _():
        for m in range(MICRO):
            swap.n2(m).wait_recv()
            hidden(R, m)
            down_sent(R, swap, m)
            down_done(R, swap, m)
            swap.hop_h(m).start()
        R.y[...] = R.ys[...]
        swap.hop_dy(0).wait_recv()
        swap.dy(0).start()
        swap.dy(0).wait_recv()
        hidden_back(R, 0)
        normed_back(R, swap, 0)
        middle_back(R, swap, 0)
        attend_back(R, tables, 0)
        stream_back(R, 0)
        swap.hop_dy(1).wait_recv()
        swap.dy(1).start()
        swap.dy(1).wait_recv()
        hidden_back(R, 1)

    @only(1)
    def _():
        def start(m):
            swap.hop_h(m).wait_recv()
            rows = own_rows(m)
            project_qkv(R, R.h, tables, rows, SEQ)
            attend(R, tables, m)
            after_attention(R, R.h, m)
            swap.n2(m).start()

        def feed(m):
            swap.n2(m).wait_recv()
            hidden(R, m)
            down_sent(R, swap, m)
            down_done(R, swap, m)
            swap.y(m).start()

        def finish(m):
            middle_back(R, swap, m)
            attend_back(R, tables, m)
            stream_back(R, m)
            swap.hop_dy(m).start()
            swap.dh(m).start()

        for m in range(MICRO):
            for move in (swap.og, swap.cos, swap.sin, swap.mask):
                move(m).wait_recv()
            swap.dy(m).start()
        start(0)
        feed(0)
        start(1)
        swap.dy(0).wait_recv()
        hidden_back(R, 0)
        normed_back(R, swap, 0)
        feed(1)
        finish(0)
        swap.dy(1).wait_recv()
        hidden_back(R, 1)
        normed_back(R, swap, 1)
        finish(1)

    wire.drain()

    def rest_a():
        only(0)(lambda: normed_back(R, swap, 1))

    def rest_b():
        only(0)(lambda: middle_back(R, swap, 1))

    def rest_c():
        only(0)(lambda: attend_back(R, tables, 1))

    def rest_d():
        @only(0)
        def _():
            stream_back(R, 1)
            R.dh[...] = R.dhs[...]

    made = set()
    start_scatter(wire, place, bufs, rest[:N_RS_SCRATCH], made, lambda *a: unpack(R, *a))
    wire.add(weight_grads(R, wire, made, (rest_a, rest_b, rest_c, rest_d)))
    wire.run()
    wire.drain()
    for m in range(MICRO):
        swap.n2(m).wait_send()
        swap.dy(m).wait_send()

    @only(0)
    def _():
        for m in range(MICRO):
            swap.hop_h(m).wait_send()

    @only(1)
    def _():
        for m in range(MICRO):
            for move in (swap.og, swap.cos, swap.sin, swap.mask, swap.y, swap.dh, swap.hop_dy):
                move(m).wait_send()
            swap.y(m).wait_recv()
            swap.dh(m).wait_recv()


N_WIRE = 208


def run_layers(ins):
    outs = [(TOK, D)] * 2 + [(14, 4864)] * 2 + [(76, D), (14, QKV), (14, D), (1, 14), (1, 18), (1, 14)]
    kinds = [BF, BF] + [F32] * 8
    vmem = pl.BlockSpec(memory_space=pltpu.VMEM)
    dma = pltpu.SemaphoreType.DMA
    return pl.pallas_call(
        layers_kernel,
        out_shape=[jax.ShapeDtypeStruct(s, k) for s, k in zip(outs, kinds)],
        in_specs=[pl.BlockSpec(memory_space=pl.ANY) if n in IN_HBM else vmem for n in INS],
        out_specs=[vmem] * len(OUTS),
        scratch_shapes=[pltpu.VMEM(s, BF) for s in bufs_shapes()]
        + [pltpu.VMEM(s, k) for _, s, k in LOCAL]
        + rs_scratch()
        + [dma((N_WIRE,)), dma((N_WIRE,)), dma((9,)), dma((N_SWAP,)), dma((N_SWAP,))],
        compiler_params=pltpu.CompilerParams(
            collective_id=0, has_side_effects=True, vmem_limit_bytes=127 * 2**19
        ),
        name="two_layers",
    )(*ins)


def rope_tables(segment_row, head_size):
    length = segment_row.shape[0]
    places = jnp.arange(length, dtype=jnp.int32)
    changes = jnp.concatenate(
        [jnp.ones((1,), jnp.int32), (segment_row[1:] != segment_row[:-1]).astype(jnp.int32)]
    )
    starts = lax.cummax(places * changes, axis=0)
    offsets = (places - starts).astype(F32)
    ladder = jnp.arange(head_size // 2, dtype=F32) * (-2.0 * math.log(rope_base) / head_size)
    angles = offsets[:, None] * jnp.exp(ladder)[None, :]
    cos, sin = jnp.cos(angles), jnp.sin(angles)
    return (
        jnp.concatenate([cos, cos, cos, cos], axis=-1),
        jnp.concatenate([-sin, sin, -sin, sin], axis=-1),
    )


def mask_of(segment_row):
    places = jnp.arange(segment_row.shape[0], dtype=jnp.int32)
    seen = (segment_row[:, None] == segment_row[None, :]) & (places[None, :] <= places[:, None])
    return jnp.where(seen, 0.0, -1e30).astype(F32)


def shards(
    tokens_in, out_grad, segments, norm1_gain, qkv_weight, qkv_bias, out_weight, norm2_gain,
    gate_weight, up_weight, down_weight,
):
    half = MICRO * SEQ
    rows = segments[:, 0]
    cos, sin = jax.vmap(rope_tables, in_axes=(0, None))(rows, HEAD_DIM)
    y, dh, g, u, d, q, o, a, b, c = run_layers([
        gate_weight[0],
        up_weight[0],
        down_weight[0],
        qkv_weight[0],
        out_weight[0],
        norm1_gain,
        qkv_bias,
        norm2_gain,
        tokens_in.reshape(half, D),
        out_grad.reshape(half, D),
        cos.reshape(half, 128),
        sin.reshape(half, 128),
        jax.vmap(mask_of)(rows),
        *constants(),
    ])
    shape = (1, MICRO, 1, SEQ, D)
    return (
        y.reshape(shape), dh.reshape(shape), a, q[None], b, o[None], c, g[None], u[None], d[None]
    )


def solution(mesh):
    in_specs = (
        P(None, "fsdp", None, None),
        P(None, "fsdp", None, None),
        P(None, "fsdp", None),
        P("section", "fsdp"),
        P("section", "fsdp", None),
        P("section", "fsdp"),
        P("section", "fsdp", None),
        P("section", "fsdp"),
        P("section", "fsdp", None),
        P("section", "fsdp", None),
        P("section", "fsdp", None),
    )
    out_specs = (
        P("section", None, "fsdp", None, None),
        P("section", None, "fsdp", None, None),
        P("section", "fsdp"),
        P("section", "fsdp", None),
        P("section", "fsdp"),
        P("section", "fsdp", None),
        P("section", "fsdp"),
        P("section", "fsdp", None),
        P("section", "fsdp", None),
        P("section", "fsdp", None),
    )
    return jax.shard_map(shards, mesh=mesh, in_specs=in_specs, out_specs=out_specs, check_vma=False)
```

profile of v0, /device:TPU:1, one launch (start us, length us, event | category | flops | bytes accessed | tf_op | source)
XLA Modules:
  0.0 302.3 jit_solution(1462016267719272894)
XLA Ops:
  0.6 0.8 slice_compare_fusion
  1.5 0.1 fusion.1
  1.6 1.5 and_select_fusion.refs_12_
  3.1 0.1 copy.43
  3.2 0.2 reduce_window_max.15
  3.4 0.1 reduce
  3.5 0.5 fusion
  4.1 1.0 pad_maximum_fusion
  5.1 284.9 %two_layers.1 = (bf16[256,896]{1,0:T(8,128)(2,1)}, bf16[256,896]{1,0:T(8,128)(2,1)}, f32[14,4864]{1,0:T(8,128)}, f32[14,4864]{1,0:T(8,128)}, f32[76,896]{1,0:T(8...) custom-call(bf16[14,4864]{1,0:T(8,128)(2,1)} %bitcast.34, ...), custom_call_target="tpu_custom_call" | custom-call | tf_op jit(solution)/shard_map/two_layers/pallas_call | solution.py:1097
  289.9 0.0 copy-start.1
  290.0 0.0 copy-start
  290.0 1.6 copy.48
  291.5 0.0 copy-start.4
  291.5 0.0 copy-start.3
  291.5 0.0 copy-start.2
  291.5 1.6 copy.47
  293.1 2.0 copy.49
  295.1 2.0 copy.50
  297.0 1.9 copy.51
  299.0 0.0 copy-done.1
  299.0 0.8 copy.57
  299.7 0.0 copy-done
  299.7 0.8 copy.58
  300.5 0.0 copy-done.4
  300.5 0.5 copy.59
  301.0 0.0 copy-done.3
  301.0 0.5 copy.60
  301.5 0.0 copy-done.2
  301.5 0.5 copy.61
  (3 shorter events, 0.0 us)
Async XLA Ops:
  289.9 9.0 %copy-start.1 = (bf16[256,896]{1,0:T(8,128)(2,1)S(1)}, bf16[256,896]{1,0:T(8,128)(2,1)}, u32[]{:S(2)}) copy-start(bf16[256,896]{1,0:T(8,128)(2,1)} %get-tuple-element.20) | copy-start | bytes 1376260
  290.0 9.8 %copy-start = (bf16[256,896]{1,0:T(8,128)(2,1)S(1)}, bf16[256,896]{1,0:T(8,128)(2,1)}, u32[]{:S(2)}) copy-start(bf16[256,896]{1,0:T(8,128)(2,1)} %get-tuple-element.21) | copy-start | bytes 1376260
  291.5 9.0 %copy-start.4 = (f32[1,14]{1,0:T(1,128)S(1)}, f32[1,14]{1,0:T(1,128)}, u32[]{:S(2)}) copy-start(f32[1,14]{1,0:T(1,128)} %get-tuple-element.77) | copy-start | bytes 172
  291.5 9.5 %copy-start.3 = (f32[1,18]{1,0:T(1,128)S(1)}, f32[1,18]{1,0:T(1,128)}, u32[]{:S(2)}) copy-start(f32[1,18]{1,0:T(1,128)} %get-tuple-element.79) | copy-start | bytes 220
  291.5 10.0 %copy-start.2 = (f32[1,14]{1,0:T(1,128)S(1)}, f32[1,14]{1,0:T(1,128)}, u32[]{:S(2)}) copy-start(f32[1,14]{1,0:T(1,128)} %get-tuple-element.81) | copy-start | bytes 172
where the time goes:
time: 308 us; the launch traced here: 302 us
  Pallas kernels  285 us (93%)
  local copies, waits for them, and re-layouts  12.2 us (4%)
  other arithmetic  4.25 us (1%)
    pallas_call x1, Pallas kernels, run_layers(): pl.pallas_call(layers_kernel, out_shape=[jax.ShapeDtypeStruct(s, k) for s...  285 us
    unnamed x20, local copies, waits for them, and re-layouts  12.1 us

commit v1 on v0

--- a/solution.py
+++ b/solution.py
@@ -635,20 +635,23 @@
     return 0.5 * jnp.tanh(0.5 * v) + 0.5
 
 
-def hidden(R, m):
-    rows = pair(m)
-
+def hidden(R, rows):
     def body(j, carry):
-        at = pl.ds(pl.multiple_of(j * 256, 256), 256)
+        at = pl.ds(pl.multiple_of(j * 1280, 1280), 1280)
         n2 = R.N2[rows]
-        gate = mm(n2, R.G[:, :, :, :, at].reshape(DP, 256))
-        up = mm(n2, R.U[:, :, :, :, at].reshape(DP, 256))
+        gate = mm(n2, R.G[:, :, :, :, at].reshape(DP, 1280))
+        up = mm(n2, R.U[:, :, :, :, at].reshape(DP, 1280))
         R.GA[rows, at] = gate.astype(BF)
         R.UP[rows, at] = up.astype(BF)
         R.ACT[rows, at] = (gate * sigmoid(gate) * up).astype(BF)
         return carry
 
-    lax.fori_loop(0, FF // 256, body, 0)
+    lax.fori_loop(0, FF // 1280, body, 0)
+
+
+def hidden_other(R, swap, m):
+    swap.n2(m).wait_recv()
+    hidden(R, pair_other(m))
 
 
 class Swap:
@@ -711,16 +714,13 @@
 
 def normed_back(R, swap, m):
     rows = pair(m)
-    R.acc[...] = jnp.zeros_like(R.acc)
-
-    def body(j, carry):
-        at = pl.ds(pl.multiple_of(j * 512, 512), 512)
-        R.acc[...] += mm_t(R.GA[rows, at], R.G[:, :, :, :, at].reshape(DP, 512)) + mm_t(
-            R.UP[rows, at], R.U[:, :, :, :, at].reshape(DP, 512)
-        )
+
+    def body(x, carry):
+        at = pl.ds(pl.multiple_of(x * 256, 256), 256)
+        R.acc[:, at] = mm_t(R.GA[rows], R.G[x].reshape(256, FF)) + mm_t(R.UP[rows], R.U[x].reshape(256, FF))
         return carry
 
-    lax.fori_loop(0, FF // 512, body, 0)
+    lax.fori_loop(0, 4, body, 0)
     R.dn[...] = R.acc[SEQ:].astype(BF)
     swap.dn(m).start()
 
@@ -881,31 +881,59 @@
     R.q_st[...] = R.q_s[...].astype(BF)
 
 
-def unpack(R, name, c, mine, other=None):
-    if name in "GU":
-        R.g_s[c] = mine.astype(F32)
-        R.g_s[1 - c] = other.astype(F32)
-        dst = R.g_o if name == "G" else R.u_o
+def keep(R, name, c, mine, other=None):
+    dst = getattr(R, name.lower() + "_o")
+    if other is None:
+        dst[...] = mine
+    else:
+        dst[c] = mine
+        dst[1 - c] = other
+
+
+def finish_kernel(y, dh, g, u, d, q, o, y_o, dh_o, a_o, q_o, b_o, o_o, c_o, g_o, u_o, d_o, wide, flat):
+    y_o[...] = y[...]
+    dh_o[...] = dh[...]
+    for src, dst in ((g, g_o), (u, u_o)):
+        wide[...] = src[...].astype(F32)
         for f in range(64):
             at = 80 * (f // 2)
-            dst[:, 76 * f:76 * f + 76] = R.g_s[f % 2, 0:14, at:at + 76]
-    elif name == "D":
-        R.acc[0:80, 0:D] = mine.astype(F32)
-        R.d_o[...] = R.acc[0:76, 0:D]
-    elif name == "O":
-        R.o_s[...] = mine.astype(F32)
-        R.o_o[...] = R.o_s[0:14]
-    else:
-        R.q_s[...] = mine.astype(F32)
-        R.q_o[...] = R.q_s[0:14]
-        R.a_o[...] = R.q_s[14:15, 0:14]
-        R.c_o[...] = R.q_s[14:15, 32:46]
-        R.b_o[...] = R.q_s[14:15, 64:82]
+            flat[0:14, 76 * f:76 * f + 76] = wide[f % 2, 0:14, at:at + 76]
+        for r in range(14):
+            dst[r] = flat[r:r + 1, :]
+    flat[0:80, 0:D] = d[...].astype(F32)
+    for r in range(76):
+        d_o[r] = flat[r:r + 1, 0:D]
+    flat[0:16, 0:QKV] = q[...].astype(F32)
+    for r in range(14):
+        q_o[r] = flat[r:r + 1, 0:QKV]
+    a_o[...] = flat[14:15, 0:14]
+    c_o[...] = flat[14:15, 32:46]
+    b_o[...] = flat[14:15, 64:82]
+    flat[16:32, 0:D] = o[...].astype(F32)
+    for r in range(14):
+        o_o[r] = flat[16 + r:17 + r, 0:D]
+
+
+def finish_grads(parts):
+    shapes = [
+        (TOK, D), (TOK, D), (1, 14), (14, 1, QKV), (1, 18), (14, 1, D), (1, 14),
+        (14, 1, 4864), (14, 1, 4864), (76, 1, D),
+    ]
+    vmem = pl.BlockSpec(memory_space=pltpu.VMEM)
+    return pl.pallas_call(
+        finish_kernel,
+        out_shape=[jax.ShapeDtypeStruct(s, BF if k < 2 else F32) for k, s in enumerate(shapes)],
+        in_specs=[vmem] * len(parts),
+        out_specs=[vmem] * len(shapes),
+        scratch_shapes=[pltpu.VMEM((2, 16, FF), F32), pltpu.VMEM((80, 4864), F32)],
+        compiler_params=pltpu.CompilerParams(vmem_limit_bytes=32 * 2**20),
+        name="finish_grads",
+    )(*parts)
 
 
 INS = ("g_in", "u_in", "d_in", "q_in", "o_in", "a_in", "b_in", "c_in", "tokens", "og", "cos", "sin", "mask") + CONST
 IN_HBM = ("og", "tokens", "cos", "sin", "mask")
-OUTS = ("y", "dh", "g_o", "u_o", "d_o", "q_o", "o_o", "a_o", "b_o", "c_o")
+OUTS = ("y", "dh", "g_o", "u_o", "d_o", "q_o", "o_o")
 LOCAL = (
     ("h", (TOK, D), BF), ("N1", (TOK, DP), BF), ("QR", (TOK, D), BF),
     ("KV", (2, 3, TOK, 128), BF), ("CP", (TOK, DP), BF),
@@ -985,12 +1013,16 @@
 
     @only(0)
     def _():
-        for m in range(MICRO):
-            swap.n2(m).wait_recv()
-            hidden(R, m)
-            down_sent(R, swap, m)
-            down_done(R, swap, m)
-            swap.hop_h(m).start()
+        hidden(R, pair_own(0))
+        hidden_other(R, swap, 0)
+        down_sent(R, swap, 0)
+        hidden(R, pair_own(1))
+        down_done(R, swap, 0)
+        swap.hop_h(0).start()
+        hidden_other(R, swap, 1)
+        down_sent(R, swap, 1)
+        down_done(R, swap, 1)
+        swap.hop_h(1).start()
         R.y[...] = R.ys[...]
         swap.hop_dy(0).wait_recv()
         swap.dy(0).start()
@@ -1016,9 +1048,11 @@
             swap.n2(m).start()
 
         def feed(m):
-            swap.n2(m).wait_recv()
-            hidden(R, m)
+            hidden(R, pair_own(m))
+            hidden_other(R, swap, m)
             down_sent(R, swap, m)
+
+        def fed(m):
             down_done(R, swap, m)
             swap.y(m).start()
 
@@ -1036,11 +1070,13 @@
         start(0)
         feed(0)
         start(1)
+        fed(0)
         swap.dy(0).wait_recv()
         hidden_back(R, 0)
         normed_back(R, swap, 0)
         feed(1)
         finish(0)
+        fed(1)
         swap.dy(1).wait_recv()
         hidden_back(R, 1)
         normed_back(R, swap, 1)
@@ -1064,7 +1100,7 @@
             R.dh[...] = R.dhs[...]
 
     made = set()
-    start_scatter(wire, place, bufs, rest[:N_RS_SCRATCH], made, lambda *a: unpack(R, *a))
+    start_scatter(wire, place, bufs, rest[:N_RS_SCRATCH], made, lambda *a: keep(R, *a))
     wire.add(weight_grads(R, wire, made, (rest_a, rest_b, rest_c, rest_d)))
     wire.run()
     wire.drain()
@@ -1090,8 +1126,8 @@
 
 
 def run_layers(ins):
-    outs = [(TOK, D)] * 2 + [(14, 4864)] * 2 + [(76, D), (14, QKV), (14, D), (1, 14), (1, 18), (1, 14)]
-    kinds = [BF, BF] + [F32] * 8
+    outs = [(TOK, D)] * 2 + [(2, 16, FF)] * 2 + [(80, D), (16, QKV), (16, D)]
+    kinds = [BF] * 7
     vmem = pl.BlockSpec(memory_space=pltpu.VMEM)
     dma = pltpu.SemaphoreType.DMA
     return pl.pallas_call(
@@ -1140,7 +1176,7 @@
     half = MICRO * SEQ
     rows = segments[:, 0]
     cos, sin = jax.vmap(rope_tables, in_axes=(0, None))(rows, HEAD_DIM)
-    y, dh, g, u, d, q, o, a, b, c = run_layers([
+    parts = run_layers([
         gate_weight[0],
         up_weight[0],
         down_weight[0],
@@ -1157,9 +1193,9 @@
         *constants(),
     ])
     shape = (1, MICRO, 1, SEQ, D)
-    return (
-        y.reshape(shape), dh.reshape(shape), a, q[None], b, o[None], c, g[None], u[None], d[None]
-    )
+    y, dh, a, q, b, o, c, g, u, d = finish_grads(parts)
+    q, o, g, u, d = [part.transpose(1, 0, 2) for part in (q, o, g, u, d)]
+    return y.reshape(shape), dh.reshape(shape), a, q, b, o, c, g, u, d
 
 
 def solution(mesh):

time: 308 us -> 311 us (level)
  the two profiles are of different devices: /device:TPU:1 before, /device:TPU:0 now
where the time goes in v1:
time: 311 us; the launch traced here: 304 us
  Pallas kernels  293 us (94%)
  local copies, waits for them, and re-layouts  6.41 us (2%)
  other arithmetic  4.25 us (1%)
    pallas_call x1, Pallas kernels, run_layers(): pl.pallas_call(layers_kernel, out_shape=[jax.ShapeDtypeStruct(s, k) for s...  291 us
    unnamed x14, local copies, waits for them, and re-layouts  6.28 us

profile of v1, /device:TPU:0, one launch (start us, length us, event | category | flops | bytes accessed | tf_op | source)
XLA Modules:
  0.0 304.4 jit_solution(15328765697965788398)
XLA Ops:
  0.6 0.8 slice_compare_fusion
  1.5 0.1 fusion.1
  1.6 1.5 and_select_fusion.refs_12_
  3.1 0.1 copy.33
  3.2 0.2 reduce_window_max.15
  3.4 0.1 reduce
  3.5 0.5 fusion
  4.1 1.0 pad_maximum_fusion
  5.1 291.0 %two_layers.1 = (bf16[256,896]{1,0:T(8,128)(2,1)}, bf16[256,896]{1,0:T(8,128)(2,1)}, bf16[2,16,2560]{2,1,0:T(8,128)(2,1)}, bf16[2,16,2560]{2,1,0:T(8,128)(2,1)},...) custom-call(bf16[14,4864]{1,0:T(8,128)(2,1)} %bitcast.29, bf16[14,4864]{1,0:T(8,128)(2,1)} %bitcast.30, ...), custom_call_target="tpu_custom_call" | custom-call | tf_op jit(solution)/shard_map/two_layers/pallas_call | solution.py:1133
  296.1 0.0 copy-start
  296.1 1.0 copy-done
  297.1 0.0 copy-start.1
  297.1 1.0 copy-done.1
  298.2 0.0 copy-start.2
  298.2 0.9 copy-done.2
  299.1 0.0 copy-start.3
  299.1 0.9 copy-done.3
  300.0 0.0 copy-start.4
  300.0 0.9 copy-done.4
  300.9 0.0 copy-start.5
  300.9 0.8 copy-done.5
  301.7 0.0 copy-start.6
  301.7 0.7 copy-done.6
  302.4 1.5 finish_grads.1
  (3 shorter events, 0.0 us)
Async XLA Ops:
  296.1 1.0 copy-start
  297.1 1.0 copy-start.1
  298.2 0.9 copy-start.2
  299.1 0.9 copy-start.3
  300.0 0.9 copy-start.4
  300.9 0.8 copy-start.5
  301.7 0.7 copy-start.6
